TPU v7x, 32 devices: a whole 2x2x4 slice. The times are simulated.
32 devices in a mesh: frame: 32 (over z, y, x, core).
Axes of the slice: x: 2, y: 2, z: 4, core: 2. Of those that a mesh axis runs over, the one named last changes fastest.
Arguments:
- diag_even: float32 [64, 256, 256], P('frame'), may hold values from -0.375 to 0.375
- inv_odd: float32 [64, 256, 256], P('frame'), as said below
- coupling: float32 [128, 256, 256], P('frame'), may hold values from -0.375 to 0.375
- arrow_blocks: float32 [128, 512, 256], P('frame'), as said below
- arrow_tip: float32 [512, 512], P('frame'), may hold values from -6 to 6
Outputs:
- diag_new: float32 [64, 256, 256], P('frame')
- couple_new: float32 [64, 256, 256], P('frame')
- arrow_new: float32 [64, 512, 256], P('frame')
- tip_new: float32 [512, 512], P('frame')
Inputs may be any that keep to these rules, and one draw needn't show every extreme that they name: `inv_odd`: each block is symmetric, with a diagonal near 1 and small off-diagonal entries. `arrow_blocks`: Real-valued entries of order 256 ** -0.5 or smaller.
All inputs are finite; a program needn't handle non-finite values.
Results may differ from a plain program's by a relative error of at most 0.000076.
Values sent between devices are 32-bit elements; how exact they have to be, the bound alone decides.
A program may use at most 64 MiB of HBM per device.

v0:
```python
import jax
import jax.numpy as jnp
from jax import lax
from jax.sharding import PartitionSpec as P


def shifted(x, axis, by):
    count = lax.axis_size(axis)
    pairs = [(i, i + by) for i in range(count) if 0 <= i + by < count]
    return lax.ppermute(x, axis, pairs)


def product(left, right):
    return jnp.matmul(left, right, precision=lax.Precision.HIGHEST)


def per_device(diag_even, inv_odd, coupling, arrow_blocks, arrow_tip):
    half_count = inv_odd.shape[0]
    order = coupling.shape[1]
    width = arrow_blocks.shape[1]
    linked = coupling.reshape(half_count, 2, order, order)
    link_prev = linked[:, 0]
    link_next = linked[:, 1]
    paired = arrow_blocks.reshape(half_count, 2, width, order)
    arrow_even = paired[:, 0]
    arrow_odd = paired[:, 1]
    left_prod = product(link_prev, inv_odd)
    arrow_inv = product(arrow_odd, inv_odd)
    diag_left = product(left_prod, jnp.swapaxes(link_prev, 1, 2))
    couple_new = -product(left_prod, link_next)
    arrow_left = product(arrow_inv, jnp.swapaxes(link_prev, 1, 2))
    tip_part = jnp.einsum("hab,hcb->ac", arrow_inv, arrow_odd, precision=lax.Precision.HIGHEST)
    inv_next = product(inv_odd, link_next)
    diag_right = product(jnp.swapaxes(link_next, 1, 2), inv_next)
    arrow_right = product(arrow_odd, inv_next)
    recv_diag, recv_arrow = shifted((diag_right[-1], arrow_right[-1]), "frame", 1)
    diag_rest = diag_right[:-1]
    arrow_rest = arrow_right[:-1]
    diag_shift = jnp.concatenate([recv_diag[None], diag_rest], axis=0)
    arrow_shift = jnp.concatenate([recv_arrow[None], arrow_rest], axis=0)
    tip_sum = lax.psum_scatter(tip_part, "frame", scatter_dimension=0, tiled=True)
    diag_new = diag_even - diag_left - diag_shift
    arrow_new = arrow_even - arrow_left - arrow_shift
    tip_new = arrow_tip - tip_sum
    return (diag_new, couple_new, arrow_new, tip_new)


def solution(mesh):
    placed = (
        P("frame", None, None),
        P("frame", None, None),
        P("frame", None, None),
        P("frame", None, None),
        P("frame", None),
    )
    return jax.shard_map(
        per_device,
        mesh=mesh,
        in_specs=placed,
        out_specs=(
            P("frame", None, None),
            P("frame", None, None),
            P("frame", None, None),
            P("frame", None),
        ),
        check_vma=False,
    )
```

profile of v0, /device:TPU:0, one launch (start us, length us, event | category | flops | bytes accessed | tf_op | source)
XLA Modules:
  0.0 159.4 jit_solution(9062245889695176454)
XLA Ops:
  7.2 0.0 copy-start
  7.2 0.0 reduce-scatter.2.cloned.1.call-start
  7.2 0.0 copy-start.2
  7.2 1.0 copy-done
  8.2 2.3 %fusion = f32[2,512,256]{2,1,0:T(8,128)S(1)} fusion(f32[2,256,256]{2,1,0:T(8,128)S(1)} %copy-done, f32[2,2,512,256]{3,2,1,0:T(8,128)} %bitcast.62), kind=kOutput, calls=%fused_computation.9 | convolution fusion | flops 805306368 | bytes 2621440 | tf_op jit(solution)/shard_map/dot_general | solution.py:14
  10.5 0.0 copy-done.2
  10.5 0.0 copy-start.1
  10.5 2.8 %convolution_bitcast_fusion = f32[512,512]{1,0:T(8,128)} fusion(f32[2,512,256]{2,1,0:T(8,128)S(1)} %fusion, f32[2,2,512,256]{3,2,1,0:T(8,128)S(1)} %bitcast.63), kind=kOutput, calls=%fused_computation | convolution fusion | flops 1610612736 | bytes 3145728 | tf_op jit(solution)/shard_map/hab,hcb->ac/dot_general | solution.py:32
  13.4 0.0 reduce-scatter.2.cloned.1.call-update
  13.4 0.0 copy-done.1
  13.4 0.0 copy-start.3
  13.4 1.0 fusion.2
  14.5 1.0 convolution_bitcast_fusion.2
  15.6 2.4 %collective-permute-start = (f32[256,256]{1,0:T(8,128)S(1)}, f32[256,256]{1,0:T(8,128)S(1)}, u32[]{:S(2)}, u32[]{:S(2)}) collective-permute-start(f32[256,256]{1,0:T(8,128)S(1)} %get-tuple-element.6), channel_id=1, source_target_pairs={{0,1},{1,2},{2,3},{3,4},{4,5},{5,6},{6,7},{7,8},{8,9},{9,10},{10,1... | collective-permute-start | bytes 786440 | tf_op jit(solution)/shard_map/ppermute | solution.py:10
  17.9 0.0 copy-done.3
  18.0 1.1 convolution_bitcast_fusion.1
  19.1 0.1 slice_bitcast_fusion.5
  19.1 0.0 copy-start.4
  19.2 4.7 %collective-permute-start.1 = (f32[512,256]{1,0:T(8,128)S(1)}, f32[512,256]{1,0:T(8,128)S(1)}, u32[]{:S(2)}, u32[]{:S(2)}) collective-permute-start(f32[512,256]{1,0:T(8,128)S(1)} %get-tuple-element.4), channel_id=1, source_target_pairs={{0,1},{1,2},{2,3},{3,4},{4,5},{5,6},{6,7},{7,8},{8,9},{9,10},{10,1... | collective-permute-start | bytes 1572872 | tf_op jit(solution)/shard_map/ppermute | solution.py:10
  23.8 0.7 fusion.1
  24.5 1.5 convolution_negate_fusion
  25.9 0.0 collective-permute-done
  25.9 0.0 copy-done.4
  25.9 1.5 maximum_subtract_fusion.1
  27.4 0.0 collective-permute-done.1
  27.4 0.0 copy-start.5
  27.4 2.1 %maximum_subtract_fusion = f32[2,512,256]{2,1,0:T(8,128)} fusion(f32[1,512,256]{2,1,0:T(8,128)S(1)} %get-tuple-element.5, f32[1,512,256]{2,1,0:T(8,128)S(1)} %bitcast.66, f32[2,512,256]{2,1,0:T(8,128)S(1)} %fusion, f32[2,2,256,256]{3,2,1,0:T(8,128)S(1)} %bitcast.61, f32[2,2,512,256]{3,2,1,0:T(8,128)S(1)} %bitcast.65), kind=kOutput, calls=%fused_computation.8 | convolution fusion | flops 806092800 | bytes 4718592 | tf_op jit(solution)/shard_map/dot_general | solution.py:14
  29.6 121.6 %reduce-scatter.2.cloned.1.call-done = f32[16,512]{1,0:T(8,128)} async-done(((f32[512,512]{1,0:T(8,128)}), f32[16,512]{1,0:T(8,128)}) %reduce-scatter.2.cloned.1.call-update) | async-done | bytes 32784 | tf_op jit(solution)/shard_map/reduce_scatter | solution.py:41
  151.2 0.0 copy-done.5
  151.2 1.4 sub.19
  (1 shorter events, 0.0 us)
Async XLA Ops:
  7.2 1.0 copy-start
  7.2 144.0 %reduce-scatter.2.cloned.1.call-start = ((), (), s32[]{:S(2)}) async-start(), calls=%async_computation.1 | async-start | bytes 1081344 | tf_op jit(solution)/shard_map/reduce_scatter | solution.py:41
  7.2 3.3 %copy-start.2 = (f32[4,512,256]{2,1,0:T(8,128)S(1)}, f32[4,512,256]{2,1,0:T(8,128)}, u32[]{:S(2)}) copy-start(f32[4,512,256]{2,1,0:T(8,128)} %param.8) | copy-start | bytes 6291460
  10.5 2.9 %copy-start.1 = (f32[4,256,256]{2,1,0:T(8,128)S(1)}, f32[4,256,256]{2,1,0:T(8,128)}, u32[]{:S(2)}) copy-start(f32[4,256,256]{2,1,0:T(8,128)} %param.7) | copy-start | bytes 3145732
  13.4 4.5 %copy-start.3 = (f32[4,512,256]{2,1,0:T(8,128)S(1)}, f32[4,512,256]{2,1,0:T(8,128)}, u32[]{:S(2)}) copy-start(f32[4,512,256]{2,1,0:T(8,128)} %param.8) | copy-start | bytes 6291460
  15.6 10.4 %collective-permute-start = (f32[256,256]{1,0:T(8,128)S(1)}, f32[256,256]{1,0:T(8,128)S(1)}, u32[]{:S(2)}, u32[]{:S(2)}) collective-permute-start(f32[256,256]{1,0:T(8,128)S(1)} %get-tuple-element.6), channel_id=1, source_target_pairs={{0,1},{1,2},{2,3},{3,4},{4,5},{5,6},{6,7},{7,8},{8,9},{9,10},{10,1... | collective-permute-start | bytes 786440 | tf_op jit(solution)/shard_map/ppermute | solution.py:10
  19.1 6.8 %copy-start.4 = (f32[2,256,256]{2,1,0:T(8,128)S(1)}, f32[2,256,256]{2,1,0:T(8,128)}, u32[]{:S(2)}) copy-start(f32[2,256,256]{2,1,0:T(8,128)} %param.5) | copy-start | bytes 1572868
  19.2 8.2 %collective-permute-start.1 = (f32[512,256]{1,0:T(8,128)S(1)}, f32[512,256]{1,0:T(8,128)S(1)}, u32[]{:S(2)}, u32[]{:S(2)}) collective-permute-start(f32[512,256]{1,0:T(8,128)S(1)} %get-tuple-element.4), channel_id=1, source_target_pairs={{0,1},{1,2},{2,3},{3,4},{4,5},{5,6},{6,7},{7,8},{8,9},{9,10},{10,1... | collective-permute-start | bytes 1572872 | tf_op jit(solution)/shard_map/ppermute | solution.py:10
  27.4 123.8 %copy-start.5 = (f32[16,512]{1,0:T(8,128)S(1)}, f32[16,512]{1,0:T(8,128)}, u32[]{:S(2)}) copy-start(f32[16,512]{1,0:T(8,128)} %param.9) | copy-start | bytes 98308
Sparse Core Ops, SparseCore 0:
  13.5 137.5 reduce-scatter.1
where the time goes:
time: 160 us; the launch traced here: 159 us
  waiting for transfers between devices  122 us (76%)
  between operations  14.2 us (9%)
  matrix products  14 us (9%)
  starting transfers between devices  7.07 us (4%)
    reduce_scatter x1, waiting for transfers between devices, per_device(): lax.psum_scatter(tip_part, 'frame', scatter_dimension=0, tiled=True)  122 us
    dot_general x8, matrix products, product(): return jnp.matmul(left, right, precision=lax.Precision.HIGHEST)  11.2 us
    ppermute x2, starting transfers between devices, shifted(): return lax.ppermute(x, axis, pairs)  7.03 us
  transfers between devices with their start and end apart: 3, of which 1 were waited for; matrix products, arithmetic and copies ran while one was open for 6% of the time, Pallas kernels for 0%

commit v1 on v0

v1 whole, which is shorter than its diff:
```python
import functools
import itertools

import jax
import jax.numpy as jnp
from jax import lax
from jax.experimental import pallas as pl
from jax.experimental.pallas import tpu as pltpu
from jax.sharding import PartitionSpec as P

F32 = jnp.float32
BF16 = jnp.bfloat16
MESH = pl.DeviceIdType.MESH


def shifted(x, axis, by):
    count = lax.axis_size(axis)
    pairs = [(i, i + by) for i in range(count) if 0 <= i + by < count]
    return lax.ppermute(x, axis, pairs)


def product(left, right):
    return jnp.matmul(left, right, precision=lax.Precision.HIGHEST)


def per_device_plain(diag_even, inv_odd, coupling, arrow_blocks, arrow_tip):
    half_count = inv_odd.shape[0]
    order = coupling.shape[1]
    width = arrow_blocks.shape[1]
    linked = coupling.reshape(half_count, 2, order, order)
    link_prev = linked[:, 0]
    link_next = linked[:, 1]
    paired = arrow_blocks.reshape(half_count, 2, width, order)
    arrow_even = paired[:, 0]
    arrow_odd = paired[:, 1]
    left_prod = product(link_prev, inv_odd)
    arrow_inv = product(arrow_odd, inv_odd)
    diag_left = product(left_prod, jnp.swapaxes(link_prev, 1, 2))
    couple_new = -product(left_prod, link_next)
    arrow_left = product(arrow_inv, jnp.swapaxes(link_prev, 1, 2))
    tip_part = jnp.einsum("hab,hcb->ac", arrow_inv, arrow_odd, precision=lax.Precision.HIGHEST)
    inv_next = product(inv_odd, link_next)
    diag_right = product(jnp.swapaxes(link_next, 1, 2), inv_next)
    arrow_right = product(arrow_odd, inv_next)
    recv_diag, recv_arrow = shifted((diag_right[-1], arrow_right[-1]), "frame", 1)
    diag_shift = jnp.concatenate([recv_diag[None], diag_right[:-1]], axis=0)
    arrow_shift = jnp.concatenate([recv_arrow[None], arrow_right[:-1]], axis=0)
    tip_sum = lax.psum_scatter(tip_part, "frame", scatter_dimension=0, tiled=True)
    return (diag_even - diag_left - diag_shift, couple_new, arrow_even - arrow_left - arrow_shift, arrow_tip - tip_sum)


def split(x):
    hi = x.astype(BF16)
    return hi, (x - hi.astype(F32)).astype(BF16)


def stage_plans(bits):
    rest = [(b,) for b in range(1, min(bits, 3))]
    far = [tuple(range(3, bits))] if bits > 3 else []
    first = [(0,)] + rest + far
    second = [(0,)] + rest[1:] + far + rest[:1]
    return [first, second]


def stage_shapes(bits, rows, cols, plan):
    shapes = []
    left = bits
    for group in plan:
        left -= len(group)
        shapes.append((2 ** len(group) - 1,) + (2,) * left + (rows, cols))
    return shapes


def kernel(cfg, diag_ref, inv_ref, coup_ref, arr_ref, tip_ref,
           diag_out, coup_out, arr_out, tip_out,
           diag_v, inv_v, coup_v, arr_v, tip_v,
           m_hi, m_lo, mp_hi, mp_lo, p_hi, p_lo, v_hi, v_lo,
           ar_buf, r_buf, ar_recv, r_recv, ar_mid, r_mid, al_buf, l_buf,
           diag_o, coup_o, arr_o, tip_o, t_buf, *tail):
    n, bits, half, order, width, rows, cols, plans = cfg
    counts = [len(p) for p in plans]
    r_bufs = []
    at = 0
    for c in counts:
        r_bufs.append(tail[at:at + c])
        at += c
    in_sem, out_sem, bs_sem, br_sem, ts_sem, tr_sem = tail[at:]

    me = lax.axis_index("frame")
    bit = [(me // (2 ** b)) % 2 for b in range(bits)]
    nxt = lax.rem(me + 1, n)
    prv = lax.rem(me + n - 1, n)

    def partner(mask):
        other = me
        for b in mask:
            other = other + (1 - 2 * bit[b]) * (2 ** b)
        return other

    def masks(group):
        res = []
        for m in range(1, 2 ** len(group)):
            res.append(tuple(b for i, b in enumerate(group) if (m >> i) & 1))
        return res

    barrier = pltpu.get_barrier_semaphore()
    greet = []
    for group in plans[0]:
        greet += [partner(m) for m in masks(group)]
    greet += [nxt, prv]
    for other in greet:
        pl.semaphore_signal(barrier, inc=1, device_id=(other,), device_id_type=MESH)

    loads = {}
    slot = itertools.count()

    def load(key, src, dst):
        copy = pltpu.make_async_copy(src, dst, in_sem.at[next(slot)])
        copy.start()
        loads[key] = copy

    order_h = list(reversed(range(half)))
    for h in order_h:
        load(("P", h), inv_ref.at[h], inv_v.at[h])
        load(("K", h), arr_ref.at[2 * h + 1], arr_v.at[2 * h + 1])
        if h == half - 1:
            load(("V", h), coup_ref.at[2 * h + 1], coup_v.at[2 * h + 1])
    for h in order_h:
        load(("U", h), coup_ref.at[2 * h], coup_v.at[2 * h])
        if h != half - 1:
            load(("V", h), coup_ref.at[2 * h + 1], coup_v.at[2 * h + 1])
    for h in order_h:
        load(("E", h), arr_ref.at[2 * h], arr_v.at[2 * h])
        load(("D", h), diag_ref.at[h], diag_v.at[h])
    load("tip", tip_ref, tip_v)

    def wait_load(key):
        loads.pop(key).wait()

    K, U, VT = pl.ds(0, width), pl.ds(width, order), pl.ds(width + order, order)

    def put_m(h, rows_at, x):
        m_hi[h, rows_at, :], m_lo[h, rows_at, :] = split(x)

    def cat_l(hi, lo):
        return jnp.concatenate([hi, lo, hi], axis=1)

    def nn(lh, ll, rh, rl):
        return lax.dot_general(cat_l(lh, ll), jnp.concatenate([rh, rh, rl], axis=0),
                               (((1,), (0,)), ((), ())), preferred_element_type=F32)

    def nt(pairs):
        left = jnp.concatenate([cat_l(p[0], p[1]) for p in pairs], axis=1)
        right = jnp.concatenate([jnp.concatenate([p[2], p[2], p[3]], axis=1) for p in pairs], axis=1)
        return lax.dot_general(left, right, (((1,), (1,)), ((), ())), preferred_element_type=F32)

    def get_p(h):
        wait_load(("P", h))
        p_hi[h], p_lo[h] = split(inv_v[h])

    def get_v(h):
        wait_load(("V", h))
        v = coup_v[2 * h + 1]
        v_hi[h], v_lo[h] = split(v)
        put_m(h, VT, v.T)

    def get_k(h):
        wait_load(("K", h))
        put_m(h, K, arr_v[2 * h + 1])

    def get_u(h):
        wait_load(("U", h))
        put_m(h, U, coup_v[2 * h])

    def times_p(h, at):
        mp_hi[h, at, :], mp_lo[h, at, :] = split(nn(m_hi[h, at, :], m_lo[h, at, :], p_hi[h], p_lo[h]))

    def times_v(h, at):
        return nn(mp_hi[h, at, :], mp_lo[h, at, :], v_hi[h], v_lo[h])

    def times_ut(h, at):
        return nt([(mp_hi[h, at, :], mp_lo[h, at, :], m_hi[h, U, :], m_lo[h, U, :])])

    last = half - 1
    get_k(last)
    get_p(last)
    times_p(last, K)
    get_v(last)
    ar_buf[...] = times_v(last, K)
    pl.semaphore_wait(barrier, len(greet))

    def boundary(src, dst, i):
        return pltpu.make_async_remote_copy(src_ref=src, dst_ref=dst, send_sem=bs_sem.at[i], recv_sem=br_sem.at[i],
                                            device_id=(nxt,), device_id_type=MESH)

    send_ar = boundary(ar_buf, ar_recv, 0)
    send_r = boundary(r_buf, r_recv, 1)

    @pl.when(me < n - 1)
    def _():
        send_ar.start()

    times_p(last, VT)
    r_buf[...] = times_v(last, VT)

    @pl.when(me < n - 1)
    def _():
        send_r.start()

    for h in order_h[1:]:
        get_k(h)
        get_p(h)
        times_p(h, K)

    def block_index(done, free, combo):
        idx = [None] * bits
        for b in done:
            idx[b] = bit[b]
        for b, v in zip(free, combo):
            idx[b] = v
        return tuple(reversed(idx))

    sem_at = [0]
    tip_sends = []

    class Chunk:
        def __init__(self, c):
            self.c, self.plan, self.stage, self.done = c, plans[c], 0, []

        def compute(self):
            c = self.c
            at = pl.ds(c * cols, cols)
            part = nt([(mp_hi[h, K, :], mp_lo[h, K, :], m_hi[h, at, :], m_lo[h, at, :]) for h in order_h])
            for d in range(n):
                where = tuple((d >> b) & 1 for b in reversed(range(bits)))
                t_buf[(c,) + where] = part[d * rows:(d + 1) * rows, :]

        def send(self):
            group = self.plan[self.stage]
            self.copies = []
            for i, mask in enumerate(masks(group)):
                idx = [slice(None)] * bits
                for b in self.done:
                    idx[b] = bit[b]
                for b in group:
                    idx[b] = (1 - bit[b]) if b in mask else bit[b]
                copy = pltpu.make_async_remote_copy(
                    src_ref=t_buf.at[(self.c,) + tuple(reversed(idx))],
                    dst_ref=r_bufs[self.c][self.stage].at[i],
                    send_sem=ts_sem.at[sem_at[0]], recv_sem=tr_sem.at[sem_at[0]],
                    device_id=(partner(mask),), device_id_type=MESH)
                sem_at[0] += 1
                copy.start()
                self.copies.append(copy)
                tip_sends.append(copy)

        def receive(self):
            group = self.plan[self.stage]
            self.done = self.done + list(group)
            free = [b for b in range(bits) if b not in self.done]
            for copy in self.copies:
                copy.wait_recv()
            got = r_bufs[self.c][self.stage]
            for combo in itertools.product((0, 1), repeat=len(free)):
                where = (self.c,) + block_index(self.done, free, combo)
                total = t_buf[where]
                for i in range(2 ** len(group) - 1):
                    total = total + got[(i,) + tuple(reversed(combo))]
                t_buf[where] = total
            self.stage += 1
            if self.stage < len(self.plan):
                self.send()

        def finish(self):
            at = pl.ds(self.c * cols, cols)
            tip_o[:, at] = tip_v[:, at] - t_buf[(self.c,) + tuple(reversed(bit))]

    chunks = [Chunk(c) for c in range(len(plans))]
    for chunk in chunks:
        chunk.compute()
        chunk.send()

    stores = []

    def store(src, dst):
        copy = pltpu.make_async_copy(src, dst, out_sem.at[len(stores)])
        copy.start()
        stores.append(copy)

    def couple(h):
        get_u(h)
        times_p(h, U)
        coup_o[h] = -times_v(h, U)
        store(coup_o.at[h], coup_out.at[h])

    def lefts(h):
        al_buf[h] = times_ut(h, K)
        l_buf[h] = times_ut(h, U)

    def rights(h):
        ar_mid[h] = times_v(h, K)
        times_p(h, VT)
        r_mid[h] = times_v(h, VT)

    def combine(h):
        wait_load(("E", h))
        wait_load(("D", h))
        arr_o[h] = arr_v[2 * h] - al_buf[h] - ar_mid[h - 1]
        store(arr_o.at[h], arr_out.at[h])
        diag_o[h] = diag_v[h] - l_buf[h] - r_mid[h - 1]
        store(diag_o.at[h], diag_out.at[h])

    pieces = []
    for h in order_h:
        if h != last:
            pieces.append(functools.partial(get_v, h))
            pieces.append(functools.partial(rights, h))
        pieces.append(functools.partial(couple, h))
        pieces.append(functools.partial(lefts, h))
    for h in order_h[:-1]:
        pieces.append(functools.partial(combine, h))
    steps = [chunk.receive for _ in range(0) for chunk in chunks]
    for s in range(max(counts)):
        steps += [chunk.receive for chunk in chunks if s < len(chunk.plan)]
    while pieces or steps:
        if pieces:
            pieces.pop(0)()
        if steps:
            steps.pop(0)()
    wait_load("tip")
    for chunk in chunks:
        chunk.finish()
    store(tip_o, tip_out)

    wait_load(("E", 0))
    wait_load(("D", 0))
    arr_o[0] = arr_v[0] - al_buf[0]
    diag_o[0] = diag_v[0] - l_buf[0]

    @pl.when(me > 0)
    def _():
        send_ar.wait_recv()
        arr_o[0] = arr_o[0] - ar_recv[...]
        send_r.wait_recv()
        diag_o[0] = diag_o[0] - r_recv[...]

    store(arr_o.at[0], arr_out.at[0])
    store(diag_o.at[0], diag_out.at[0])

    @pl.when(me < n - 1)
    def _():
        send_ar.wait_send()
        send_r.wait_send()

    for copy in tip_sends:
        copy.wait_send()
    for copy in stores:
        copy.wait()


def per_device(n, diag_even, inv_odd, coupling, arrow_blocks, arrow_tip):
    half, order = inv_odd.shape[:2]
    width = arrow_blocks.shape[1]
    rows = arrow_tip.shape[0]
    bits = n.bit_length() - 1
    if 2 ** bits != n or bits < 3 or rows % 8 or width % (2 * 128):
        return per_device_plain(diag_even, inv_odd, coupling, arrow_blocks, arrow_tip)
    plans = stage_plans(bits)
    cols = width // len(plans)
    cfg = (n, bits, half, order, width, rows, cols, plans)
    shapes = [s for plan in plans for s in stage_shapes(bits, rows, cols, plan)]
    copies = sum(2 ** len(g) - 1 for plan in plans for g in plan)
    tall = width + 2 * order
    vmem = pltpu.VMEM
    scratch = [
        vmem(diag_even.shape, F32), vmem(inv_odd.shape, F32), vmem(coupling.shape, F32), vmem(arrow_blocks.shape, F32),
        vmem(arrow_tip.shape, F32),
        vmem((half, tall, order), BF16), vmem((half, tall, order), BF16),
        vmem((half, tall, order), BF16), vmem((half, tall, order), BF16),
        vmem((half, order, order), BF16), vmem((half, order, order), BF16),
        vmem((half, order, order), BF16), vmem((half, order, order), BF16),
        vmem((width, order), F32), vmem((order, order), F32), vmem((width, order), F32), vmem((order, order), F32),
        vmem((half, width, order), F32), vmem((half, order, order), F32),
        vmem((half, width, order), F32), vmem((half, order, order), F32),
        vmem((half, order, order), F32), vmem((half, order, order), F32), vmem((half, width, order), F32),
        vmem(arrow_tip.shape, F32),
        vmem((len(plans),) + (2,) * bits + (rows, cols), F32),
    ]
    scratch += [vmem(s, F32) for s in shapes]
    dma = pltpu.SemaphoreType.DMA
    scratch += [dma((6 * half + 1,)), dma((3 * half + 1,)), dma((2,)), dma((2,)), dma((copies,)), dma((copies,))]
    anywhere = pl.BlockSpec(memory_space=pl.ANY)
    return pl.pallas_call(
        functools.partial(kernel, cfg),
        out_shape=(
            jax.ShapeDtypeStruct((half, order, order), F32),
            jax.ShapeDtypeStruct((half, order, order), F32),
            jax.ShapeDtypeStruct((half, width, order), F32),
            jax.ShapeDtypeStruct(arrow_tip.shape, F32),
        ),
        in_specs=[anywhere] * 5,
        out_specs=(anywhere,) * 4,
        scratch_shapes=scratch,
        compiler_params=pltpu.CompilerParams(collective_id=0, has_side_effects=True, vmem_limit_bytes=48 * 2 ** 20),
        cost_estimate=pl.CostEstimate(flops=90 * 2 * order ** 3, bytes_accessed=6 * 2 ** 20, transcendentals=0),
    )(diag_even, inv_odd, coupling, arrow_blocks, arrow_tip)


def solution(mesh):
    blocks = P("frame", None, None)
    tip = P("frame", None)
    return jax.shard_map(
        functools.partial(per_device, mesh.shape["frame"]),
        mesh=mesh,
        in_specs=(blocks, blocks, blocks, blocks, tip),
        out_specs=(blocks, blocks, blocks, tip),
        check_vma=False,
    )
```

time: 160 us -> 35.4 us (0.22)
  waiting for transfers between devices: 122 us -> 0 us
  Pallas kernels: 0 us -> 27.2 us
  matrix products: 14 us -> 0 us
  between operations: 14.2 us -> 0.65 us
  starting transfers between devices: 7.07 us -> 0 us
  local copies, waits for them, and re-layouts: 1.12 us -> 7.23 us
    reduce_scatter x1 -> x0, waiting for transfers between devices: 122 us -> none  [per_device(): lax.psum_scatter(tip_part, 'frame', scatter_dimension=0, tiled=True)]
    pallas_call x0 -> x1, Pallas kernels: none -> 27.2 us  [per_device(): pl.pallas_call(functools.partial(kernel, cfg), out_shape=(jax.ShapeDtypeS...]
    dot_general x9 -> x0, matrix products: 14 us -> none  [the longest x8 11.2 us: product(): return jnp.matmul(left, right, precision=lax.Precision.HIGHEST)]
    ppermute x2 -> x0, starting transfers between devices: 7.03 us -> none  [shifted(): return lax.ppermute(x, axis, pairs)]
    unnamed x12, local copies, waits for them, and re-layouts: 1.01 us -> 7.23 us
  transfers between devices with their start and end apart: 3 -> 0, of which waited for: 1 -> 0; matrix products, arithmetic and copies ran while one was open for 6% -> 0% of each run, Pallas kernels for 0% -> 0%
where the time goes in v1:
time: 35.4 us; the launch traced here: 35 us
  Pallas kernels  27.2 us (77%)
  local copies, waits for them, and re-layouts  7.23 us (20%)
  between operations  0.65 us (2%)
    pallas_call x1, Pallas kernels, per_device(): pl.pallas_call(functools.partial(kernel, cfg), out_shape=(jax.ShapeDtypeS...  27.2 us
    unnamed x12, local copies, waits for them, and re-layouts  7.23 us

profile of v1, /device:TPU:0, one launch (start us, length us, event | category | flops | bytes accessed | tf_op | source)
XLA Modules:
  0.0 35.0 jit_solution(13439903113268946734)
XLA Ops:
  0.6 0.0 copy-start
  0.6 1.2 %copy-done = f32[4,256,256]{2,1,0:T(8,128)S(1)} copy-done((f32[4,256,256]{2,1,0:T(8,128)S(1)}, f32[4,256,256]{2,1,0:T(8,128)}, u32[]{:S(2)}) %copy-start) | copy-done | bytes 1048600
  1.9 0.0 copy-start.1
  1.9 1.0 %copy-done.1 = f32[2,256,256]{2,1,0:T(8,128)S(1)} copy-done((f32[2,256,256]{2,1,0:T(8,128)S(1)}, f32[2,256,256]{2,1,0:T(8,128)}, u32[]{:S(2)}) %copy-start.1) | copy-done | bytes 524312
  2.9 0.0 copy-start.2
  2.9 1.0 %copy-done.2 = f32[2,256,256]{2,1,0:T(8,128)S(1)} copy-done((f32[2,256,256]{2,1,0:T(8,128)S(1)}, f32[2,256,256]{2,1,0:T(8,128)}, u32[]{:S(2)}) %copy-start.2) | copy-done | bytes 524312
  3.9 0.0 copy-start.3
  3.9 0.8 %copy-done.3 = f32[16,512]{1,0:T(8,128)S(1)} copy-done((f32[16,512]{1,0:T(8,128)S(1)}, f32[16,512]{1,0:T(8,128)}, u32[]{:S(2)}) %copy-start.3) | copy-done | bytes 32792
  4.7 27.2 %shard_map.84 = (f32[2,256,256]{2,1,0:T(8,128)S(1)}, f32[2,256,256]{2,1,0:T(8,128)S(1)}, f32[2,512,256]{2,1,0:T(8,128)S(1)}, f32[16,512]{1,0:T(8,128)S(1)}) custom-call(f32[2,256,256]{2,1,0:T(8,128)S(1)} %copy-done.1, f32[2,256,256]{2,1,0:T(8,128)S(1)} %copy-done.2, f32[4,256,256]{2,1,0:T(8,128)S(1)} %copy-done, f32[4,512,256]{2,1,0:T(8,128)} %arr_ref.1, ...), custom_call_target="tpu_custom_call" | custom-call | flops 3019898880 | bytes 6291456 | tf_op jit(solution)/shard_map/pallas_call | solution.py:393
  31.9 0.8 %copy.13 = f32[2,256,256]{2,1,0:T(8,128)} copy(f32[2,256,256]{2,1,0:T(8,128)S(1)} %get-tuple-element.8) | data formatting | bytes 1048576
  32.7 0.8 %copy.14 = f32[2,256,256]{2,1,0:T(8,128)} copy(f32[2,256,256]{2,1,0:T(8,128)S(1)} %get-tuple-element.9) | data formatting | bytes 1048576
  33.4 1.0 %copy.15 = f32[2,512,256]{2,1,0:T(8,128)} copy(f32[2,512,256]{2,1,0:T(8,128)S(1)} %get-tuple-element.10) | data formatting | bytes 2097152
  34.4 0.6 %copy.16 = f32[16,512]{1,0:T(8,128)} copy(f32[16,512]{1,0:T(8,128)S(1)} %get-tuple-element.11) | data formatting | bytes 65536
Async XLA Ops:
  0.6 1.2 %copy-start = (f32[4,256,256]{2,1,0:T(8,128)S(1)}, f32[4,256,256]{2,1,0:T(8,128)}, u32[]{:S(2)}) copy-start(f32[4,256,256]{2,1,0:T(8,128)} %coup_ref.1) | copy-start | bytes 3145732
  1.9 1.0 %copy-start.1 = (f32[2,256,256]{2,1,0:T(8,128)S(1)}, f32[2,256,256]{2,1,0:T(8,128)}, u32[]{:S(2)}) copy-start(f32[2,256,256]{2,1,0:T(8,128)} %diag_ref.1) | copy-start | bytes 1572868
  2.9 1.0 %copy-start.2 = (f32[2,256,256]{2,1,0:T(8,128)S(1)}, f32[2,256,256]{2,1,0:T(8,128)}, u32[]{:S(2)}) copy-start(f32[2,256,256]{2,1,0:T(8,128)} %inv_ref.1) | copy-start | bytes 1572868
  3.9 0.8 %copy-start.3 = (f32[16,512]{1,0:T(8,128)S(1)}, f32[16,512]{1,0:T(8,128)}, u32[]{:S(2)}) copy-start(f32[16,512]{1,0:T(8,128)} %tip_ref.1) | copy-start | bytes 98308

commit v2 on v1

--- a/solution.py
+++ b/solution.py
@@ -11,6 +11,7 @@
 F32 = jnp.float32
 BF16 = jnp.bfloat16
 MESH = pl.DeviceIdType.MESH
+AHEAD = 1
 
 
 def shifted(x, axis, by):
@@ -55,11 +56,8 @@
 
 
 def stage_plans(bits):
-    rest = [(b,) for b in range(1, min(bits, 3))]
-    far = [tuple(range(3, bits))] if bits > 3 else []
-    first = [(0,)] + rest + far
-    second = [(0,)] + rest[1:] + far + rest[:1]
-    return [first, second]
+    core, one, two, far = (0,), (1,), (2,), tuple(range(3, bits))
+    return [[core, two, far, one],[core, two, far, one], [core, far, two, one], [core, far, two, one]]
 
 
 def stage_shapes(bits, rows, cols, plan):
@@ -72,11 +70,11 @@
 
 
 def kernel(cfg, diag_ref, inv_ref, coup_ref, arr_ref, tip_ref,
-           diag_out, coup_out, arr_out, tip_out,
+           diag_o, coup_o, arr_o, tip_o,
            diag_v, inv_v, coup_v, arr_v, tip_v,
            m_hi, m_lo, mp_hi, mp_lo, p_hi, p_lo, v_hi, v_lo,
            ar_buf, r_buf, ar_recv, r_recv, ar_mid, r_mid, al_buf, l_buf,
-           diag_o, coup_o, arr_o, tip_o, t_buf, *tail):
+           t_buf, *tail):
     n, bits, half, order, width, rows, cols, plans = cfg
     counts = [len(p) for p in plans]
     r_bufs = []
@@ -84,7 +82,7 @@
     for c in counts:
         r_bufs.append(tail[at:at + c])
         at += c
-    in_sem, out_sem, bs_sem, br_sem, ts_sem, tr_sem = tail[at:]
+    in_sem, bs_sem, br_sem, ts_sem, tr_sem = tail[at:]
 
     me = lax.axis_index("frame")
     bit = [(me // (2 ** b)) % 2 for b in range(bits)]
@@ -105,8 +103,8 @@
 
     barrier = pltpu.get_barrier_semaphore()
     greet = []
-    for group in plans[0]:
-        greet += [partner(m) for m in masks(group)]
+    for mask in sorted({m for plan in plans for group in plan for m in masks(group)}):
+        greet.append(partner(mask))
     greet += [nxt, prv]
     for other in greet:
         pl.semaphore_signal(barrier, inc=1, device_id=(other,), device_id_type=MESH)
@@ -200,13 +198,6 @@
     def _():
         send_ar.start()
 
-    times_p(last, VT)
-    r_buf[...] = times_v(last, VT)
-
-    @pl.when(me < n - 1)
-    def _():
-        send_r.start()
-
     for h in order_h[1:]:
         get_k(h)
         get_p(h)
@@ -226,14 +217,6 @@
     class Chunk:
         def __init__(self, c):
             self.c, self.plan, self.stage, self.done = c, plans[c], 0, []
-
-        def compute(self):
-            c = self.c
-            at = pl.ds(c * cols, cols)
-            part = nt([(mp_hi[h, K, :], mp_lo[h, K, :], m_hi[h, at, :], m_lo[h, at, :]) for h in order_h])
-            for d in range(n):
-                where = tuple((d >> b) & 1 for b in reversed(range(bits)))
-                t_buf[(c,) + where] = part[d * rows:(d + 1) * rows, :]
 
         def send(self):
             group = self.plan[self.stage]
@@ -276,22 +259,28 @@
             tip_o[:, at] = tip_v[:, at] - t_buf[(self.c,) + tuple(reversed(bit))]
 
     chunks = [Chunk(c) for c in range(len(plans))]
-    for chunk in chunks:
-        chunk.compute()
-        chunk.send()
-
-    stores = []
-
-    def store(src, dst):
-        copy = pltpu.make_async_copy(src, dst, out_sem.at[len(stores)])
-        copy.start()
-        stores.append(copy)
+    wide = max(cols, min(order, width // 2))
+    for first in range(0, width, wide):
+        at = pl.ds(first, wide)
+        part = nt([(mp_hi[h, K, :], mp_lo[h, K, :], m_hi[h, at, :], m_lo[h, at, :]) for h in order_h])
+        for c in range(first // cols, (first + wide) // cols):
+            here = slice(c * cols - first, (c + 1) * cols - first)
+            for d in range(n):
+                where = tuple((d >> b) & 1 for b in reversed(range(bits)))
+                t_buf[(c,) + where] = part[d * rows:(d + 1) * rows, here]
+            chunks[c].send()
+
+    times_p(last, VT)
+    r_buf[...] = times_v(last, VT)
+
+    @pl.when(me < n - 1)
+    def _():
+        send_r.start()
 
     def couple(h):
         get_u(h)
         times_p(h, U)
         coup_o[h] = -times_v(h, U)
-        store(coup_o.at[h], coup_out.at[h])
 
     def lefts(h):
         al_buf[h] = times_ut(h, K)
@@ -306,9 +295,7 @@
         wait_load(("E", h))
         wait_load(("D", h))
         arr_o[h] = arr_v[2 * h] - al_buf[h] - ar_mid[h - 1]
-        store(arr_o.at[h], arr_out.at[h])
         diag_o[h] = diag_v[h] - l_buf[h] - r_mid[h - 1]
-        store(diag_o.at[h], diag_out.at[h])
 
     pieces = []
     for h in order_h:
@@ -319,18 +306,18 @@
         pieces.append(functools.partial(lefts, h))
     for h in order_h[:-1]:
         pieces.append(functools.partial(combine, h))
-    steps = [chunk.receive for _ in range(0) for chunk in chunks]
+    steps = []
     for s in range(max(counts)):
         steps += [chunk.receive for chunk in chunks if s < len(chunk.plan)]
     while pieces or steps:
+        for _ in range(AHEAD):
+            if steps:
+                steps.pop(0)()
         if pieces:
             pieces.pop(0)()
-        if steps:
-            steps.pop(0)()
     wait_load("tip")
     for chunk in chunks:
         chunk.finish()
-    store(tip_o, tip_out)
 
     wait_load(("E", 0))
     wait_load(("D", 0))
@@ -344,8 +331,6 @@
         send_r.wait_recv()
         diag_o[0] = diag_o[0] - r_recv[...]
 
-    store(arr_o.at[0], arr_out.at[0])
-    store(diag_o.at[0], diag_out.at[0])
 
     @pl.when(me < n - 1)
     def _():
@@ -354,7 +339,13 @@
 
     for copy in tip_sends:
         copy.wait_send()
-    for copy in stores:
+
+
+def writer(*refs):
+    copies = [pltpu.make_async_copy(refs[i], refs[4 + i], refs[8].at[i]) for i in range(4)]
+    for copy in copies:
+        copy.start()
+    for copy in copies:
         copy.wait()
 
 
@@ -363,7 +354,7 @@
     width = arrow_blocks.shape[1]
     rows = arrow_tip.shape[0]
     bits = n.bit_length() - 1
-    if 2 ** bits != n or bits < 3 or rows % 8 or width % (2 * 128):
+    if 2 ** bits != n or bits < 4 or rows % 8 or width % (2 * 128):
         return per_device_plain(diag_even, inv_odd, coupling, arrow_blocks, arrow_tip)
     plans = stage_plans(bits)
     cols = width // len(plans)
@@ -382,28 +373,35 @@
         vmem((width, order), F32), vmem((order, order), F32), vmem((width, order), F32), vmem((order, order), F32),
         vmem((half, width, order), F32), vmem((half, order, order), F32),
         vmem((half, width, order), F32), vmem((half, order, order), F32),
-        vmem((half, order, order), F32), vmem((half, order, order), F32), vmem((half, width, order), F32),
-        vmem(arrow_tip.shape, F32),
         vmem((len(plans),) + (2,) * bits + (rows, cols), F32),
     ]
     scratch += [vmem(s, F32) for s in shapes]
     dma = pltpu.SemaphoreType.DMA
-    scratch += [dma((6 * half + 1,)), dma((3 * half + 1,)), dma((2,)), dma((2,)), dma((copies,)), dma((copies,))]
+    scratch += [dma((6 * half + 1,)), dma((2,)), dma((2,)), dma((copies,)), dma((copies,))]
     anywhere = pl.BlockSpec(memory_space=pl.ANY)
-    return pl.pallas_call(
+    inside = pl.BlockSpec(memory_space=pltpu.VMEM)
+    results = pl.pallas_call(
         functools.partial(kernel, cfg),
         out_shape=(
-            jax.ShapeDtypeStruct((half, order, order), F32),
-            jax.ShapeDtypeStruct((half, order, order), F32),
-            jax.ShapeDtypeStruct((half, width, order), F32),
-            jax.ShapeDtypeStruct(arrow_tip.shape, F32),
+            vmem((half, order, order), F32),
+            vmem((half, order, order), F32),
+            vmem((half, width, order), F32),
+            vmem(arrow_tip.shape, F32),
         ),
         in_specs=[anywhere] * 5,
-        out_specs=(anywhere,) * 4,
+        out_specs=(inside,) * 4,
         scratch_shapes=scratch,
         compiler_params=pltpu.CompilerParams(collective_id=0, has_side_effects=True, vmem_limit_bytes=48 * 2 ** 20),
         cost_estimate=pl.CostEstimate(flops=90 * 2 * order ** 3, bytes_accessed=6 * 2 ** 20, transcendentals=0),
-    )(diag_even, inv_odd, coupling, arrow_blocks, arrow_tip)
+    )(*[pltpu.with_memory_space_constraint(x, pltpu.HBM)
+        for x in (diag_even, inv_odd, coupling, arrow_blocks, arrow_tip)])
+    return pl.pallas_call(
+        writer,
+        out_shape=tuple(pltpu.HBM(r.shape, F32) for r in results),
+        in_specs=[inside] * 4,
+        out_specs=(anywhere,) * 4,
+        scratch_shapes=[dma((4,))],
+    )(*[pltpu.with_memory_space_constraint(r, pltpu.VMEM) for r in results])
 
 
 def solution(mesh):

time: 35.4 us -> 27.4 us (0.77)
  local copies, waits for them, and re-layouts: 7.23 us -> 0 us
  Pallas kernels: 27.2 us -> 26.3 us
    unnamed x12 -> x0, local copies, waits for them, and re-layouts: 7.23 us -> none
    pallas_call x1 -> x2, Pallas kernels: 27.2 us -> 26.3 us  [the longest x1 25 us: per_device(): pl.pallas_call(functools.partial(kernel, cfg), out_shape=(vmem((half, ord...]
where the time goes in v2:
time: 27.4 us; the launch traced here: 26.9 us
  Pallas kernels  26.3 us (96%)
  between operations  0.64 us (2%)
    pallas_call x1, Pallas kernels, per_device(): pl.pallas_call(functools.partial(kernel, cfg), out_shape=(vmem((half, ord...  25 us
    pallas_call x1, Pallas kernels, per_device(): pl.pallas_call(writer, out_shape=tuple((pltpu.HBM(r.shape, F32) for r in...  1.35 us

profile of v2, /device:TPU:0, one launch (start us, length us, event | category | flops | bytes accessed | tf_op | source)
XLA Modules:
  0.0 26.9 jit_solution(14423147383145571645)
XLA Ops:
  0.6 25.0 %shard_map.84 = (f32[2,256,256]{2,1,0:T(8,128)S(1)}, f32[2,256,256]{2,1,0:T(8,128)S(1)}, f32[2,512,256]{2,1,0:T(8,128)S(1)}, f32[16,512]{1,0:T(8,128)S(1)}) custom-call(f32[2,256,256]{2,1,0:T(8,128)} %diag_ref.1, f32[2,256,256]{2,1,0:T(8,128)} %inv_ref.1, f32[4,256,256]{2,1,0:T(8,128)} %coup_ref.1, f32[4,512,256]{2,1,0:T(8,128)} %arr_ref.1, f32[16,512]{1,0:T(8,128)} %tip_ref.1), custom_call_target="tpu_custom_call" | custom-call | flops 3019898880 | bytes 6291456 | tf_op jit(solution)/shard_map/pallas_call | solution.py:383
  25.6 1.4 %shard_map.85 = (f32[2,256,256]{2,1,0:T(8,128)}, f32[2,256,256]{2,1,0:T(8,128)}, f32[2,512,256]{2,1,0:T(8,128)}, f32[16,512]{1,0:T(8,128)}) custom-call(f32[2,256,256]{2,1,0:T(8,128)S(1)} %get-tuple-element.8.refs_0_, f32[2,256,256]{2,1,0:T(8,128)S(1)} %get-tuple-element.9.refs_1_, f32[2,512,256]{2,1,0:T(8,128)S(1)} %get-tuple-element.10.refs_2_, ...), custom_call_target="tpu_custom_call" | custom-call | tf_op jit(solution)/shard_map/pallas_call | solution.py:398
